TPU v7x, 32 devices: a whole 2x2x4 slice. The times are simulated.
32 devices in a mesh: grp: 2 (over x), lat: 16 (over z, y, core).
Axes of the slice: x: 2, y: 2, z: 4, core: 2. Of those that a mesh axis runs over, the one named last changes fastest.
Arguments:
- features: bfloat16 [2, 32, 192, 512], P('grp', 'lat'), parts along dimension 0, may hold values from -120 to 120
- noise_index: int32 [2], P('grp'), parts along dimension 0, may hold values from 0 to 17
- sigma_table: float32 [18], replicated, may hold values from 0.002 to 80
- affine_weight: bfloat16 [128, 1024], replicated, may hold values from -0.5 to 0.5
- norm_gain: float32 [3, 512], replicated, may hold values from 0.1 to 1.9
- norm_bias: float32 [3, 512], replicated, may hold values from -3 to 3
- conv1_weight: bfloat16 [3, 3, 512, 512], replicated, may hold values from -0.09375 to 0.09375
- conv2_weight: bfloat16 [3, 3, 512, 512], replicated, may hold values from -0.09375 to 0.09375
- conv_bias: float32 [2, 512], replicated, may hold values from -3 to 3
- qkv_weight: bfloat16 [512, 1536], replicated, may hold values from -3 to 3
- proj_weight: bfloat16 [512, 512], replicated, may hold values from -0.25 to 0.25
- proj_bias: float32 [512], replicated, may hold values from -3 to 3
Outputs:
- bottleneck: bfloat16 [2, 16, 96, 512], P('grp', 'lat'), parts along dimension 0
There are 2 independent parts, one for each index of `grp`. A program takes and returns all parts, laid end to end along the dimension named above; an argument that names none is the same for every part. Nothing has to cross between parts.
All inputs are finite; a program needn't handle non-finite values.
Results may differ from a plain program's by a relative error of at most 0.012.
The roundings to bfloat16 on the way count: a program that leaves them out, or rounds other values in their place, can miss the bound.
Values may be sent and summed in bfloat16 or wider, within the bound.
A program may use at most 128 MiB of HBM per device.

v0:
```python
import math
import jax
import jax.numpy as jnp
from jax import lax
from jax.sharding import PartitionSpec as P

HEAD_DIM = 64
GROUPS = 32
FREQS = 64
eps = 1e-05
skip_gain = 0.7071067811865476


def with_halo(block, sides, width):
    for axis, dim in sides:
        count = lax.axis_size(axis)
        forward = [(i, i + 1) for i in range(count - 1)]
        backward = [(target, source) for source, target in forward]
        low = lax.ppermute(
            lax.slice_in_dim(block, block.shape[dim] - width, None, axis=dim), axis, forward
        )
        high = lax.ppermute(lax.slice_in_dim(block, 0, width, axis=dim), axis, backward)
        block = jnp.concatenate([low, block, high], axis=dim)
    return block


def noise_terms(noise_index, sigma_table, affine_weight):
    levels_count = sigma_table.shape[0]
    chosen = (noise_index[:, None] == jnp.arange(levels_count, dtype=jnp.int32)[None, :]).astype(
        jnp.float32
    )
    sigmas = jnp.sum(chosen * sigma_table[None, :], axis=1)
    log_level = jnp.log(sigmas) / 4.0
    frequency = jnp.exp(-math.log(10000.0) * jnp.arange(FREQS, dtype=jnp.float32) / FREQS)
    angles = log_level[:, None] * frequency[None, :]
    fourier = jnp.concatenate([jnp.cos(angles), jnp.sin(angles)], axis=1).astype(jnp.bfloat16)
    affine = jnp.dot(fourier, affine_weight, preferred_element_type=jnp.float32)
    channels = affine.shape[1] // 2
    return (affine[:, :channels], affine[:, channels:])


def band_moments(values):
    members, height, breadth, channels = values.shape
    group_width = channels // GROUPS
    entries = height * breadth * group_width * lax.axis_size("lat")
    column_sums = jnp.sum(values, axis=(1, 2)).reshape(members, GROUPS, group_width).sum(axis=2)
    column_squares = (
        jnp.sum(jnp.square(values), axis=(1, 2)).reshape(members, GROUPS, group_width).sum(axis=2)
    )
    totals, squares = lax.psum((column_sums, column_squares), "lat")
    center = totals / entries
    spread = squares / entries - center * center
    return (center, spread)


def normalize(values, center, spread, norm_scale, norm_offset):
    group_width = values.shape[-1] // GROUPS
    center_full = jnp.repeat(center, group_width, axis=1)[:, None, None, :]
    factor_full = jnp.repeat(lax.rsqrt(spread + eps), group_width, axis=1)[:, None, None, :]
    return (values - center_full) * factor_full * norm_scale + norm_offset


def convolve(values, kernel):
    return lax.conv_general_dilated(
        values,
        kernel,
        (1, 1),
        ((0, 0), (1, 1)),
        dimension_numbers=("NHWC", "HWIO", "NHWC"),
        preferred_element_type=jnp.float32,
    )


def with_rims(values):
    return with_halo(values, (("lat", 1),), 1)


def key_span(total_rows, breadth):
    row_limit = max(1, 1024 // breadth)
    return math.gcd(total_rows, 1 << row_limit.bit_length() - 1)


def accumulate(running, queries, key_block, value_block):
    blended, largest, totals = running
    scores = jnp.einsum(
        "mqhd,mkhd->mqhk", queries, key_block, preferred_element_type=jnp.float32
    ) * HEAD_DIM ** (-0.5)
    rising = jnp.maximum(largest, jnp.max(scores, axis=-1))
    fading = jnp.exp(largest - rising)
    weights = jnp.exp(scores - rising[..., None])
    totals = totals * fading + jnp.sum(weights, axis=-1)
    blended = blended * fading[..., None] + jnp.einsum(
        "mqhk,mkhd->mqhd",
        weights.astype(jnp.bfloat16),
        value_block,
        preferred_element_type=jnp.float32,
    )
    return (blended, rising, totals)


def local(
    features,
    noise_index,
    sigma_table,
    affine_weight,
    norm_gain,
    norm_bias,
    conv1_weight,
    conv2_weight,
    conv_bias,
    qkv_weight,
    proj_weight,
    proj_bias,
):
    film_scale, film_shift = noise_terms(noise_index, sigma_table, affine_weight)
    film_scale = film_scale[:, None, None, :]
    film_shift = film_shift[:, None, None, :]
    source = features.astype(jnp.float32)
    center, spread = band_moments(source)
    active = jax.nn.silu(normalize(source, center, spread, norm_gain[0], norm_bias[0])).astype(
        jnp.bfloat16
    )
    first_conv = convolve(with_rims(active), conv1_weight) + conv_bias[0]
    center, spread = band_moments(first_conv)
    middle = jax.nn.silu(
        normalize(first_conv, center, spread, norm_gain[1], norm_bias[1]) * (1.0 + film_scale)
        + film_shift
    ).astype(jnp.bfloat16)
    second_conv = convolve(with_rims(middle), conv2_weight)
    level_one = ((source + second_conv + conv_bias[1]) * skip_gain).astype(jnp.bfloat16)
    level_one = lax.optimization_barrier(level_one)
    members, height, breadth, channels = level_one.shape
    low_rows = height // 2
    breadth_low = breadth // 2
    pooled = jnp.mean(
        level_one.astype(jnp.float32).reshape(members, low_rows, 2, breadth_low, 2, channels),
        axis=(2, 4),
    )
    center, spread = band_moments(pooled)
    normed = normalize(pooled, center, spread, norm_gain[2], norm_bias[2]).astype(jnp.bfloat16)
    tokens = low_rows * breadth_low
    head_count = channels // HEAD_DIM
    flat_rows = normed.reshape(members * tokens, channels)
    all_rows = low_rows * lax.axis_size("lat")
    span_rows = key_span(all_rows, breadth_low)
    span_count = all_rows // span_rows
    running = (
        jnp.zeros((members, tokens, head_count, HEAD_DIM), jnp.float32),
        jnp.full((members, tokens, head_count), -1e30, jnp.float32),
        jnp.zeros((members, tokens, head_count), jnp.float32),
    )
    projected = jnp.dot(flat_rows, qkv_weight, preferred_element_type=jnp.float32).astype(
        jnp.bfloat16
    )
    projected = projected.reshape(members, low_rows, breadth_low, 3, channels)
    queries = projected[:, :, :, 0].reshape(members, tokens, head_count, HEAD_DIM)
    key_all, value_all = (
        lax.all_gather(projected[:, :, :, 1], "lat", axis=1, tiled=True),
        lax.all_gather(projected[:, :, :, 2], "lat", axis=1, tiled=True),
    )

    def key_span_step(step_index, inner_state):
        key_slab = lax.dynamic_slice_in_dim(key_all, step_index * span_rows, span_rows, 1).reshape(
            members, span_rows * breadth_low, head_count, HEAD_DIM
        )
        value_slab = lax.dynamic_slice_in_dim(
            value_all, step_index * span_rows, span_rows, 1
        ).reshape(members, span_rows * breadth_low, head_count, HEAD_DIM)
        return accumulate(inner_state, queries, key_slab, value_slab)

    running = lax.fori_loop(0, span_count, key_span_step, running)
    blended, largest, totals = running
    attended = (
        (blended / totals[..., None]).reshape(members * tokens, channels).astype(jnp.bfloat16)
    )
    output_proj = jnp.dot(attended, proj_weight, preferred_element_type=jnp.float32) + proj_bias
    return ((pooled + output_proj.reshape(pooled.shape)) * skip_gain).astype(jnp.bfloat16)


def solution(mesh):
    return jax.shard_map(
        local,
        mesh=mesh,
        in_specs=(
            P("grp", "lat", None, None),
            P("grp"),
            P(),
            P(),
            P(),
            P(),
            P(),
            P(),
            P(),
            P(),
            P(),
            P(),
        ),
        out_specs=P("grp", "lat", None, None),
        check_vma=False,
    )
```

profile of v0, /device:TPU:0, one launch (start us, length us, event | category | flops | bytes accessed | tf_op | source)
XLA Modules:
  0.0 249.0 jit_solution(6614196855762687472)
XLA Ops:
  6.5 1.2 convert_reduce_fusion
  7.8 0.8 fusion.72
  8.6 0.8 fusion.73
  9.8 34.9 %all-reduce.2 = (f32[1,32]{1,0:T(1,128)S(1)}, f32[1,32]{1,0:T(1,128)S(1)}) all-reduce(f32[1,32]{1,0:T(1,128)S(1)} %bitcast.170, f32[1,32]{1,0:T(1,128)S(1)} %bitcast.168), channel_id=1, replica_groups=mesh['grp'=2,'lat'=16] {'lat'}, use_global_device_ids=true, to_apply=%region_5.0 | all-reduce | flops 64 | bytes 512 | tf_op jit(solution)/shard_map/psum | solution.py:50
  45.1 1.3 fusion.45
  46.4 1.3 collective-permute-start
  47.7 1.3 collective-permute-start.1
  49.6 1.3 fusion.57
  51.8 0.8 fusion.74
  52.5 1.1 fusion.58
  55.0 1.2 copy-done.7
  56.2 2.2 select_reduce_fusion.1
  58.7 30.7 %all-reduce.1 = (f32[1,32]{1,0:T(1,128)S(1)}, f32[1,32]{1,0:T(1,128)S(1)}) all-reduce(f32[1,32]{1,0:T(1,128)S(1)} %bitcast.171, f32[1,32]{1,0:T(1,128)S(1)} %bitcast.167), channel_id=1, replica_groups=mesh['grp'=2,'lat'=16] {'lat'}, use_global_device_ids=true, to_apply=%region_11.12 | all-reduce | flops 64 | bytes 512 | tf_op jit(solution)/shard_map/psum | solution.py:50
  90.6 1.3 collective-permute-start.2
  92.6 1.5 collective-permute-start.3
  94.7 1.5 collective-permute-done.3
  96.2 1.3 maximum_bitcast_fusion.1
  98.0 4.4 %convolution_select_fusion = f32[2,8,25,512]{3,1,2,0:T(8,128)S(1)} fusion(bf16[3,3,512,512]{3,2,1,0:T(8,128)(2,1)} %param.21, bf16[4,1,7,2,512]{4,2,3,0,1:T(8,128)(2,1)S(1)} %slice.92, bf16[4,1,8,25,512]{4,2,3,0,1:T(8,128)(2,1)S(1)} %copy.102, pred[8,25]{0,1:T(8,128)(4,1)S(1)} %copy-done.8), kind=kOutput, calls=%fused_computation.30 | convolution fusion | flops 1890295808 | bytes 6414536 | tf_op jit(solution)/shard_map/conv_general_dilated | solution.py:64
  104.9 34.2 %all-reduce = (f32[1,32]{1,0:T(1,128)S(1)}, f32[1,32]{1,0:T(1,128)S(1)}) all-reduce(f32[1,32]{1,0:T(1,128)S(1)} %bitcast.169, f32[1,32]{1,0:T(1,128)S(1)} %bitcast.166), channel_id=1, replica_groups=mesh['grp'=2,'lat'=16] {'lat'}, use_global_device_ids=true, to_apply=%region_20.21 | all-reduce | flops 64 | bytes 512 | tf_op jit(solution)/shard_map/psum | solution.py:50
  142.1 36.1 %all-gather.7.cloned.1.call-done = bf16[1,16,96,1,512]{4,2,3,0,1:T(8,128)(2,1)} async-done(((bf16[1,1,96,1,512]{4,2,3,0,1:T(8,128)(2,1)}), bf16[1,16,96,1,512]{4,2,3,0,1:T(8,128)(2,1)}) %all-gather.7.cloned.1.call-update) | async-done | bytes 1572880 | tf_op jit(solution)/shard_map/all_gather | solution.py:159
  178.2 40.9 %all-gather.5.cloned.1.call-done = bf16[1,16,96,1,512]{4,2,3,0,1:T(8,128)(2,1)} async-done(((bf16[1,1,96,1,512]{4,2,3,0,1:T(8,128)(2,1)}), bf16[1,16,96,1,512]{4,2,3,0,1:T(8,128)(2,1)}) %all-gather.5.cloned.1.call-update) | async-done | bytes 1572880 | tf_op jit(solution)/shard_map/all_gather | solution.py:158
  219.1 20.1 %while.18 = (s32[]{:T(128)}, f32[1,96,8,64]{1,3,2,0:T(8,128)}, f32[1,96,8]{1,2,0:T(8,128)S(1)}, f32[1,96,8]{1,2,0:T(8,128)S(1)}, bf16[1,16,96,512]{3,2,1,0:T(8,1...) while((s32[]{:T(128)}, f32[1,96,8,64]{1,3,2,0:T(8,128)}, ...), condition=%wide.region_24.25_spmd.clone, body=%wide.region_21.24_spmd.clone.sunk | while | flops 155865600 | bytes 23347460 | solution.py:171
  219.1 2.4 constant_dynamic-slice_fusion.3
  221.5 1.7 copy.121
  223.2 1.8 reshape.314
  225.7 0.9 reshape.315
  229.2 2.4 constant_dynamic-slice_fusion.3
  231.6 1.7 copy.121
  233.3 1.8 reshape.314
  235.8 0.9 reshape.315
  239.2 1.0 divide_convert_fusion
  240.2 2.0 fusion.24
  (109 shorter events, 17.0 us)
Async XLA Ops:
  6.5 132.9 %copy-start = (bf16[512,1536]{1,0:T(8,128)(2,1)S(1)}, bf16[512,1536]{1,0:T(8,128)(2,1)}, u32[]{:S(2)}) copy-start(bf16[512,1536]{1,0:T(8,128)(2,1)} %param.23) | copy-start | bytes 4718596
  6.5 171.7 %all-gather.7.cloned.1.call-start = ((), (), s32[]{:S(2)}) async-start(), calls=%async_computation.1 | async-start | bytes 1671168 | tf_op jit(solution)/shard_map/all_gather | solution.py:159
  46.4 7.3 %collective-permute-start = (bf16[1,1,192,512]{3,2,1,0:T(8,128)(2,1)S(1)}, bf16[1,1,192,512]{3,2,1,0:T(8,128)(2,1)S(1)}, u32[]{:S(2)}, u32[]{:S(2)}) collective-permute-start(bf16[1,1,192,512]{3,2,1,0:T(8,128)(2,1)S(1)} %get-tuple-element.235), channel_id=1, source_target_pairs={{0,1},{1,2},{2,3},{3,4},{4,5},{5,6},{6,7},{7,8},{8,9},{9,10},{10,1... | collective-permute-start | bytes 589832 | tf_op jit(solution)/shard_map/ppermute | solution.py:19
  47.7 6.0 %collective-permute-start.1 = (bf16[1,1,192,512]{3,2,1,0:T(8,128)(2,1)S(1)}, bf16[1,1,192,512]{3,2,1,0:T(8,128)(2,1)S(1)}, u32[]{:S(2)}, u32[]{:S(2)}) collective-permute-start(bf16[1,1,192,512]{3,2,1,0:T(8,128)(2,1)S(1)} %get-tuple-element.236), channel_id=1, source_target_pairs={{1,0},{2,1},{3,2},{4,3},{5,4},{6,5},{7,6},{8,7},{9,8},{10,9},{11,1... | collective-permute-start | bytes 589832 | tf_op jit(solution)/shard_map/ppermute | solution.py:22
  53.8 2.3 copy-start.7
  53.8 2.3 copy-start.8
  90.6 3.7 %collective-permute-start.2 = (bf16[1,1,192,512]{3,2,1,0:T(8,128)(2,1)S(1)}, bf16[1,1,192,512]{3,2,1,0:T(8,128)(2,1)S(1)}, u32[]{:S(2)}, u32[]{:S(2)}) collective-permute-start(bf16[1,1,192,512]{3,2,1,0:T(8,128)(2,1)S(1)} %slice.88), channel_id=1, source_target_pairs={{0,1},{1,2},{2,3},{3,4},{4,5},{5,6},{6,7},{7,8},{8,9},{9,10},{10,1... | collective-permute-start | bytes 589832 | tf_op jit(solution)/shard_map/ppermute | solution.py:19
  92.6 3.6 %collective-permute-start.3 = (bf16[1,1,192,512]{3,1,2,0:T(2,128)(2,1)S(1)}, bf16[1,1,192,512]{3,1,2,0:T(2,128)(2,1)S(1)}, u32[]{:S(2)}, u32[]{:S(2)}) collective-permute-start(bf16[1,1,192,512]{3,1,2,0:T(2,128)(2,1)S(1)} %slice.91), channel_id=1, source_target_pairs={{1,0},{2,1},{3,2},{4,3},{5,4},{6,5},{7,6},{8,7},{9,8},{10,9},{11,1... | collective-permute-start | bytes 589832 | tf_op jit(solution)/shard_map/ppermute | solution.py:22
  102.5 1.0 copy-start.4
  104.4 37.4 %copy-start.5 = (f32[96,512]{1,0:T(8,128)}, f32[96,512]{1,0:T(8,128)S(1)}, u32[]{:S(2)}) copy-start(f32[96,512]{1,0:T(8,128)S(1)} %reduce_sum.173) | copy-start | bytes 589828
  141.1 78.0 %all-gather.5.cloned.1.call-start = ((), (), s32[]{:S(2)}) async-start(), calls=%async_computation | async-start | bytes 1671168 | tf_op jit(solution)/shard_map/all_gather | solution.py:158
  219.1 21.1 %copy-start.6 = (f32[512]{0:T(512)S(1)}, f32[512]{0:T(512)}, u32[]{:S(2)}) copy-start(f32[512]{0:T(512)} %param.25) | copy-start | bytes 6148
  226.6 1.1 copy-start.1
  226.6 1.2 copy-start.2
  228.5 0.7 copy-start.3
  236.6 1.1 copy-start.1
  236.6 1.2 copy-start.2
  238.5 0.7 copy-start.3
Sparse Core Ops, SparseCore 0:
  141.3 36.9 all-gather.6
  180.5 38.5 all-gather.4
where the time goes:
time: 250 us; the launch traced here: 249 us
  blocking collectives  99.9 us (40%)
  waiting for transfers between devices  78.6 us (31%)
  local copies, waits for them, and re-layouts  27.8 us (11%)
  between operations  15.2 us (6%)
  matrix products  12.7 us (5%)
  other arithmetic  9.37 us (4%)
  starting transfers between devices  5.41 us (2%)
    psum x3, blocking collectives, band_moments(): totals, squares = lax.psum((column_sums, column_squares), 'lat')  99.9 us
    all_gather x1, waiting for transfers between devices, local(): lax.all_gather(projected[:, :, :, 1], 'lat', axis=1, tiled=True)  40.9 us
    all_gather x1, waiting for transfers between devices, local(): lax.all_gather(projected[:, :, :, 2], 'lat', axis=1, tiled=True)  36.1 us
    dynamic_slice x4, local copies, waits for them, and re-layouts, key_span_step(): lax.dynamic_slice_in_dim(value_all, step_index * span_rows, span_rows, 1)  8.14 us
    conv_general_dilated x2, matrix products, convolve(): lax.conv_general_dilated(values, kernel, (1, 1), ((0, 0), (1, 1)), dimens...  6.59 us
    another operation x4, local copies, waits for them, and re-layouts  5.28 us
  transfers between devices with their start and end apart: 6, of which 3 were waited for; matrix products, arithmetic and copies ran while one was open for 2% of the time, Pallas kernels for 0%

commit v1 on v0

--- a/solution.py
+++ b/solution.py
@@ -9,6 +9,18 @@
 FREQS = 64
 eps = 1e-05
 skip_gain = 0.7071067811865476
+
+
+def collect(x, axis, dim):
+    ways, here = (lax.axis_size(axis), lax.axis_index(axis))
+    grown, reach = (x, 1)
+    while reach < ways:
+        theirs = lax.ppermute(grown, axis, [(d, d ^ reach) for d in range(ways)])
+        mine_first = jnp.concatenate([grown, theirs], axis=dim)
+        theirs_first = jnp.concatenate([theirs, grown], axis=dim)
+        grown = jnp.where(here & reach == 0, mine_first, theirs_first)
+        reach = 2 * reach
+    return grown
 
 
 def with_halo(block, sides, width):
@@ -155,7 +167,7 @@
     projected = projected.reshape(members, low_rows, breadth_low, 3, channels)
     queries = projected[:, :, :, 0].reshape(members, tokens, head_count, HEAD_DIM)
     key_all, value_all = (
-        lax.all_gather(projected[:, :, :, 1], "lat", axis=1, tiled=True),
+        collect(projected[:, :, :, 1], "lat", 1),
         lax.all_gather(projected[:, :, :, 2], "lat", axis=1, tiled=True),
     )
 

time: 250 us -> 236 us (0.944)
  waiting for transfers between devices: 78.6 us -> 63.6 us
  other arithmetic: 9.37 us -> 12.8 us
    ppermute x0 -> x4, waiting for transfers between devices: none -> 62 us  [collect(): theirs = lax.ppermute(grown, axis, [(d, d ^ reach) for d in range(ways)])]
    all_gather x1 -> x0, waiting for transfers between devices: 40.9 us -> none  [local(): lax.all_gather(projected[:, :, :, 1], 'lat', axis=1, tiled=True)]
    all_gather x1, waiting for transfers between devices: 36.1 us -> 0.01 us  [local(): lax.all_gather(projected[:, :, :, 2], 'lat', axis=1, tiled=True)]
    select_n x0 -> x6, other arithmetic: none -> 3.91 us  [collect(): grown = jnp.where(here & reach == 0, mine_first, theirs_first)]
  transfers between devices with their start and end apart: 6 -> 9, of which waited for: 3 -> 5; matrix products, arithmetic and copies ran while one was open for 2% -> 3% of each run, Pallas kernels for 0% -> 0%
where the time goes in v1:
time: 236 us
  blocking collectives  100 us (42%)
  waiting for transfers between devices  63.6 us (27%)
  local copies, waits for them, and re-layouts  26.4 us (11%)
  between operations  15.3 us (6%)
  other arithmetic  12.8 us (5%)
  matrix products  11.7 us (5%)
  starting transfers between devices  5.62 us (2%)
    psum x3, blocking collectives, band_moments(): totals, squares = lax.psum((column_sums, column_squares), 'lat')  100 us
    ppermute x4, waiting for transfers between devices, collect(): theirs = lax.ppermute(grown, axis, [(d, d ^ reach) for d in range(ways)])  62 us
    dynamic_slice x4, local copies, waits for them, and re-layouts, key_span_step(): lax.dynamic_slice_in_dim(value_all, step_index * span_rows, span_rows, 1)  8.14 us
    conv_general_dilated x2, matrix products, convolve(): lax.conv_general_dilated(values, kernel, (1, 1), ((0, 0), (1, 1)), dimens...  6.58 us
    another operation x4, local copies, waits for them, and re-layouts  5.28 us
  transfers between devices with their start and end apart: 9, of which 5 were waited for; matrix products, arithmetic and copies ran while one was open for 3% of the time, Pallas kernels for 0%

profile of v1, /device:TPU:0, one launch (start us, length us, event | category | flops | bytes accessed | tf_op | source)
XLA Modules:
  0.0 235.6 jit_solution(724710143272817583)
XLA Ops:
  6.6 1.3 convert_reduce_fusion
  7.8 0.8 fusion.73
  9.9 34.9 %all-reduce.2 = (f32[1,32]{1,0:T(1,128)S(1)}, f32[1,32]{1,0:T(1,128)S(1)}) all-reduce(f32[1,32]{1,0:T(1,128)S(1)} %bitcast.190, f32[1,32]{1,0:T(1,128)S(1)} %bitcast.188), channel_id=1, replica_groups=mesh['grp'=2,'lat'=16] {'lat'}, use_global_device_ids=true, to_apply=%region_5.0 | all-reduce | flops 64 | bytes 512 | tf_op jit(solution)/shard_map/psum | solution.py:62
  45.1 1.3 fusion.45
  46.4 1.3 collective-permute-start
  47.7 1.3 collective-permute-start.1
  52.7 1.2 copy-done.9
  53.9 2.2 select_reduce_fusion.1
  56.5 30.7 %all-reduce.1 = (f32[1,32]{1,0:T(1,128)S(1)}, f32[1,32]{1,0:T(1,128)S(1)}) all-reduce(f32[1,32]{1,0:T(1,128)S(1)} %bitcast.191, f32[1,32]{1,0:T(1,128)S(1)} %bitcast.187), channel_id=1, replica_groups=mesh['grp'=2,'lat'=16] {'lat'}, use_global_device_ids=true, to_apply=%region_11.12 | all-reduce | flops 64 | bytes 512 | tf_op jit(solution)/shard_map/psum | solution.py:62
  88.3 1.3 collective-permute-start.2
  90.3 1.5 collective-permute-start.3
  92.4 1.5 collective-permute-done.3
  93.9 1.3 maximum_bitcast_fusion.1
  95.8 4.4 %convolution_select_fusion = f32[2,8,25,512]{3,1,2,0:T(8,128)S(1)} fusion(bf16[3,3,512,512]{3,2,1,0:T(8,128)(2,1)} %param.21, bf16[4,1,7,2,512]{4,2,3,0,1:T(8,128)(2,1)S(1)} %slice.92, bf16[4,1,8,25,512]{4,2,3,0,1:T(8,128)(2,1)S(1)} %copy.101, pred[8,25]{0,1:T(8,128)(4,1)S(1)} %copy-done.11), kind=kOutput, calls=%fused_computation.31 | convolution fusion | flops 1890295808 | bytes 6414536 | tf_op jit(solution)/shard_map/conv_general_dilated | solution.py:76
  102.6 34.5 %all-reduce = (f32[1,32]{1,0:T(1,128)S(1)}, f32[1,32]{1,0:T(1,128)S(1)}) all-reduce(f32[1,32]{1,0:T(1,128)S(1)} %bitcast.189, f32[1,32]{1,0:T(1,128)S(1)} %bitcast.186), channel_id=1, replica_groups=mesh['grp'=2,'lat'=16] {'lat'}, use_global_device_ids=true, to_apply=%region_20.21 | all-reduce | flops 64 | bytes 512 | tf_op jit(solution)/shard_map/psum | solution.py:62
  139.2 1.3 collective-permute-done.4
  140.6 7.9 %collective-permute-done.5 = bf16[1,2,96,512]{3,2,1,0:T(8,128)(2,1)S(1)} collective-permute-done((bf16[1,2,96,512]{3,2,1,0:T(8,128)(2,1)S(1)}, bf16[1,2,96,512]{3,2,1,0:T(8,128)(2,1)S(1)}, u32[]{:S(2)}, u32[]{:S(2)}) %collective-permute-start.5) | collective-permute-done | bytes 196640 | tf_op jit(solution)/shard_map/ppermute | solution.py:18
  148.7 11.4 %collective-permute-done.6 = bf16[1,4,96,512]{3,2,1,0:T(8,128)(2,1)S(1)} collective-permute-done((bf16[1,4,96,512]{3,2,1,0:T(8,128)(2,1)S(1)}, bf16[1,4,96,512]{3,2,1,0:T(8,128)(2,1)S(1)}, u32[]{:S(2)}, u32[]{:S(2)}) %collective-permute-start.6) | collective-permute-done | bytes 393248 | tf_op jit(solution)/shard_map/ppermute | solution.py:18
  160.1 1.0 maximum_select_fusion.2
  161.4 41.5 %collective-permute-done.7 = bf16[1,8,96,512]{3,2,1,0:T(8,128)(2,1)} collective-permute-done((bf16[1,8,96,512]{3,2,1,0:T(8,128)(2,1)}, bf16[1,8,96,512]{3,2,1,0:T(8,128)(2,1)}, u32[]{:S(2)}, u32[]{:S(2)}) %collective-permute-start.7) | collective-permute-done | bytes 786464 | tf_op jit(solution)/shard_map/ppermute | solution.py:18
  202.9 2.8 %maximum_select_fusion = bf16[1,16,96,512]{3,2,1,0:T(8,128)(2,1)} fusion(bf16[1,8,96,512]{3,2,1,0:T(8,128)(2,1)} %collective-permute-done.7, bf16[1,8,96,512]{3,2,1,0:T(8,128)(2,1)S(1)} %fusion.50, pred[]{:T(512)S(6)} %eq.26), kind=kLoop, calls=%fused_computation.26 | loop fusion | flops 2359296 | bytes 3145729 | tf_op jit(solution)/shard_map/jit(_where)/select_n | solution.py:21
  205.7 20.1 %while.18 = (s32[]{:T(128)}, f32[1,96,8,64]{1,3,2,0:T(8,128)}, f32[1,96,8]{1,2,0:T(8,128)S(1)}, f32[1,96,8]{1,2,0:T(8,128)S(1)}, bf16[1,16,96,512]{3,2,1,0:T(8,1...) while((s32[]{:T(128)}, f32[1,96,8,64]{1,3,2,0:T(8,128)}, ...), condition=%wide.region_24.25_spmd.clone, body=%wide.region_21.24_spmd.clone.sunk | while | flops 155865600 | bytes 23347460 | solution.py:183
  205.7 2.4 %constant_dynamic-slice_fusion.3 = (bf16[1,8,96,512]{3,2,1,0:T(8,128)(2,1)}, bf16[1,8,96,512]{3,2,1,0:T(8,128)(2,1)S(1)}) fusion(bf16[1,16,96,512]{3,2,1,0:T(8,128)(2,1)} %get-tuple-element.341, s32[]{:T(128)S(6)} %select_n.153, bf16[1,16,96,512]{3,2,1,0:T(8,128)(2,1)} %get-tuple-element.339), kind=kLoop, calls=%fused_computation.19.clone.1 | loop fusion | bytes 3145732 | tf_op jit(solution)/shard_map/while/body/eval_jaxpr/dynamic_slice | solution.py:178
  208.1 1.7 copy.124
  209.8 1.8 reshape.733
  212.3 0.9 reshape.734
  215.8 2.4 %constant_dynamic-slice_fusion.3 = (bf16[1,8,96,512]{3,2,1,0:T(8,128)(2,1)}, bf16[1,8,96,512]{3,2,1,0:T(8,128)(2,1)S(1)}) fusion(bf16[1,16,96,512]{3,2,1,0:T(8,128)(2,1)} %get-tuple-element.341, s32[]{:T(128)S(6)} %select_n.153, bf16[1,16,96,512]{3,2,1,0:T(8,128)(2,1)} %get-tuple-element.339), kind=kLoop, calls=%fused_computation.19.clone.1 | loop fusion | bytes 3145732 | tf_op jit(solution)/shard_map/while/body/eval_jaxpr/dynamic_slice | solution.py:178
  218.2 1.7 copy.124
  219.8 1.8 reshape.733
  222.3 0.9 reshape.734
  225.8 1.0 divide_convert_fusion
  226.8 2.0 fusion.24
  (128 shorter events, 18.5 us)
Async XLA Ops:
  6.5 130.8 %copy-start = (bf16[512,1536]{1,0:T(8,128)(2,1)S(1)}, bf16[512,1536]{1,0:T(8,128)(2,1)}, u32[]{:S(2)}) copy-start(bf16[512,1536]{1,0:T(8,128)(2,1)} %param.23) | copy-start | bytes 4718596
  6.5 43.2 %copy-start.10 = (f32[18]{0:T(128)S(1)}, f32[18]{0:T(128)}, u32[]{:S(2)}) copy-start(f32[18]{0:T(128)} %param.16) | copy-start | bytes 220
  6.5 44.6 %copy-start.7 = (f32[2,512]{1,0:T(2,128)S(1)}, f32[2,512]{1,0:T(2,128)}, u32[]{:S(2)}) copy-start(f32[2,512]{1,0:T(2,128)} %param.22) | copy-start | bytes 12292
  6.5 44.7 %copy-start.6 = (bf16[128,1024]{1,0:T(8,128)(2,1)S(1)}, bf16[128,1024]{1,0:T(8,128)(2,1)}, u32[]{:S(2)}) copy-start(bf16[128,1024]{1,0:T(8,128)(2,1)} %param.17) | copy-start | bytes 786436
  6.5 199.1 %all-gather.3.cloned.1.call-start = ((), (), s32[]{:S(2)}) async-start(), calls=%async_computation | async-start | bytes 1671168 | tf_op jit(solution)/shard_map/all_gather | solution.py:171
  46.4 5.0 %collective-permute-start = (bf16[1,1,192,512]{3,2,1,0:T(8,128)(2,1)S(1)}, bf16[1,1,192,512]{3,2,1,0:T(8,128)(2,1)S(1)}, u32[]{:S(2)}, u32[]{:S(2)}) collective-permute-start(bf16[1,1,192,512]{3,2,1,0:T(8,128)(2,1)S(1)} %get-tuple-element.235), channel_id=1, source_target_pairs={{0,1},{1,2},{2,3},{3,4},{4,5},{5,6},{6,7},{7,8},{8,9},{9,10},{10,1... | collective-permute-start | bytes 589832 | tf_op jit(solution)/shard_map/ppermute | solution.py:31
  47.7 3.7 %collective-permute-start.1 = (bf16[1,1,192,512]{3,2,1,0:T(8,128)(2,1)S(1)}, bf16[1,1,192,512]{3,2,1,0:T(8,128)(2,1)S(1)}, u32[]{:S(2)}, u32[]{:S(2)}) collective-permute-start(bf16[1,1,192,512]{3,2,1,0:T(8,128)(2,1)S(1)} %get-tuple-element.236), channel_id=1, source_target_pairs={{1,0},{2,1},{3,2},{4,3},{5,4},{6,5},{7,6},{8,7},{9,8},{10,9},{11,1... | collective-permute-start | bytes 589832 | tf_op jit(solution)/shard_map/ppermute | solution.py:34
  51.5 2.3 copy-start.9
  52.2 1.7 copy-start.11
  88.3 3.7 %collective-permute-start.2 = (bf16[1,1,192,512]{3,2,1,0:T(8,128)(2,1)S(1)}, bf16[1,1,192,512]{3,2,1,0:T(8,128)(2,1)S(1)}, u32[]{:S(2)}, u32[]{:S(2)}) collective-permute-start(bf16[1,1,192,512]{3,2,1,0:T(8,128)(2,1)S(1)} %slice.88), channel_id=1, source_target_pairs={{0,1},{1,2},{2,3},{3,4},{4,5},{5,6},{6,7},{7,8},{8,9},{9,10},{10,1... | collective-permute-start | bytes 589832 | tf_op jit(solution)/shard_map/ppermute | solution.py:31
  90.3 3.6 %collective-permute-start.3 = (bf16[1,1,192,512]{3,1,2,0:T(2,128)(2,1)S(1)}, bf16[1,1,192,512]{3,1,2,0:T(2,128)(2,1)S(1)}, u32[]{:S(2)}, u32[]{:S(2)}) collective-permute-start(bf16[1,1,192,512]{3,1,2,0:T(2,128)(2,1)S(1)} %slice.91), channel_id=1, source_target_pairs={{1,0},{2,1},{3,2},{4,3},{5,4},{6,5},{7,6},{8,7},{9,8},{10,9},{11,1... | collective-permute-start | bytes 589832 | tf_op jit(solution)/shard_map/ppermute | solution.py:34
  100.2 1.0 copy-start.4
  102.1 36.3 %copy-start.5 = (f32[96,512]{1,0:T(8,128)}, f32[96,512]{1,0:T(8,128)S(1)}, u32[]{:S(2)}) copy-start(f32[96,512]{1,0:T(8,128)S(1)} %reduce_sum.173) | copy-start | bytes 589828
  139.1 1.4 collective-permute-start.4
  140.5 8.0 %collective-permute-start.5 = (bf16[1,2,96,512]{3,2,1,0:T(8,128)(2,1)S(1)}, bf16[1,2,96,512]{3,2,1,0:T(8,128)(2,1)S(1)}, u32[]{:S(2)}, u32[]{:S(2)}) collective-permute-start(bf16[1,2,96,512]{3,2,1,0:T(8,128)(2,1)S(1)} %maximum_select_fusion.6), channel_id=1, source_target_pairs={{0,2},{1,3},{2,0},{3,1},{4,6},{5,7},{6,4},{7,5},{8,10},{9,11},{10,... | collective-permute-start | bytes 589832 | tf_op jit(solution)/shard_map/ppermute | solution.py:18
  148.5 11.6 %collective-permute-start.6 = (bf16[1,4,96,512]{3,2,1,0:T(8,128)(2,1)S(1)}, bf16[1,4,96,512]{3,2,1,0:T(8,128)(2,1)S(1)}, u32[]{:S(2)}, u32[]{:S(2)}) collective-permute-start(bf16[1,4,96,512]{3,2,1,0:T(8,128)(2,1)S(1)} %maximum_select_fusion.4), channel_id=1, source_target_pairs={{0,4},{1,5},{2,6},{3,7},{4,0},{5,1},{6,2},{7,3},{8,12},{9,13},{10,... | collective-permute-start | bytes 1179656 | tf_op jit(solution)/shard_map/ppermute | solution.py:18
  161.1 41.8 %collective-permute-start.7 = (bf16[1,8,96,512]{3,2,1,0:T(8,128)(2,1)}, bf16[1,8,96,512]{3,2,1,0:T(8,128)(2,1)}, u32[]{:S(2)}, u32[]{:S(2)}) collective-permute-start(bf16[1,8,96,512]{3,2,1,0:T(8,128)(2,1)} %maximum_select_fusion.2), channel_id=1, source_target_pairs={{0,8},{1,9},{2,10},{3,11},{4,12},{5,13},{6,14},{7,15},{8,0},{9,1},... | collective-permute-start | bytes 2359304 | tf_op jit(solution)/shard_map/ppermute | solution.py:18
  205.7 21.1 %copy-start.8 = (f32[512]{0:T(512)S(1)}, f32[512]{0:T(512)}, u32[]{:S(2)}) copy-start(f32[512]{0:T(512)} %param.25) | copy-start | bytes 6148
  213.2 1.1 copy-start.1
  213.2 1.2 copy-start.2
  215.0 0.7 copy-start.3
  223.2 1.1 copy-start.1
  223.2 1.2 copy-start.2
  225.1 0.7 copy-start.3
Sparse Core Ops, SparseCore 0:
  139.2 65.2 all-gather.2
